TPU v7x, 32 devices: a whole 2x2x4 slice. The times are simulated.
32 devices in a mesh: groups: 2 (over x), inst: 8 (over z, y), space: 2 (over core).
Axes of the slice: x: 2, y: 2, z: 4, core: 2. Of those that a mesh axis runs over, the one named last changes fastest.
Arguments:
- flow: float32 [16, 5, 64, 1024], P(('groups', 'inst'), None, 'space'), parts along dimension 0, may hold values from -4 to 15, as said below
- grid_velocity: float32 [16, 2, 64, 1024], P(('groups', 'inst'), None, 'space'), parts along dimension 0, may hold values from -0.4 to 0.4
- cell_volume: float32 [64, 1024], P('space'), may hold values from 0.5 to 2
Outputs:
- flow_next: float32 [16, 5, 64, 1024], P(('groups', 'inst'), None, 'space'), parts along dimension 0
- mean_flow: float32 [10, 64, 1024], P('groups', 'space', 'inst'), parts along dimension 0
There are 2 independent parts, one for each index of `groups`. A program takes and returns all parts, laid end to end along the dimension named above; an argument that names none is the same for every part. Nothing has to cross between parts.
Inputs may be any that keep to these rules, and one draw needn't show every extreme that they name: `flow`: each cell's state has density and implied pressure between 0.3 and 3, and speeds of at most 1.2 along each direction.
All inputs are finite; a program needn't handle non-finite values.
Results may differ from a plain program's by a relative error of at most 0.00005.
Values sent between devices are 32-bit elements; how exact they have to be, the bound alone decides.
A program may use at most 128 MiB of HBM per device.

v0:
```python
import math

import jax
import jax.numpy as jnp
import numpy as np
from jax import lax
from jax.sharding import PartitionSpec as P

gamma_ratio = 1.4
courant_number = 1.5
section_weight = 0.5


def extended_2(x, sides, width):
    for axis, dim in sides:
        devices, length = (lax.axis_size(axis), x.shape[dim])
        up = [(i, (i + 1) % devices) for i in range(devices)]
        down = [(j, i) for i, j in up]
        last = lax.slice_in_dim(x, length - width, length, axis=dim)
        leading = lax.slice_in_dim(x, 0, width, axis=dim)
        before = lax.ppermute(last, axis, up)
        after = lax.ppermute(leading, axis, down)
        x = jnp.concatenate([before, x, after], axis=dim)
    return x


def coefficient(offsets, inst_count):
    parity = (offsets % 2).astype(jnp.float32)
    angle = math.pi / inst_count * offsets.astype(jnp.float32)
    safe_sine = jnp.where(offsets == 0, 1.0, jnp.sin(angle))
    value = (1.0 - 2.0 * parity) * (math.pi / inst_count) * jnp.cos(angle) / safe_sine
    return jnp.where(offsets == 0, 0.0, value)


def cell_state(state):
    density = state[:, 0]
    velocity = state[:, 1:4] / density[:, None]
    kinetic = 0.5 * jnp.sum(state[:, 1:4] * velocity, axis=1)
    pressure = (gamma_ratio - 1.0) * (state[:, 4] - kinetic)
    sound = jnp.sqrt(gamma_ratio * pressure / density)
    return (velocity, pressure, sound)


def side_flux(state, face_speed, normal):
    velocity, pressure, sound = cell_state(state)
    normal_speed = velocity[:, normal]
    relative = normal_speed - face_speed
    unit_push = jnp.asarray(np.eye(5, dtype=np.float32)[1 + normal]).reshape(1, 5, 1, 1)
    unit_work = jnp.asarray(np.eye(5, dtype=np.float32)[4]).reshape(1, 5, 1, 1)
    flux = (
        state * relative[:, None]
        + pressure[:, None] * unit_push
        + (pressure * normal_speed)[:, None] * unit_work
    )
    return (flux, jnp.abs(relative) + sound)


def face_flux(left_state, right_state, left_grid, right_grid, normal):
    face_speed = 0.5 * (left_grid[:, normal] + right_grid[:, normal])
    flux_left, reach_left = side_flux(left_state, face_speed, normal)
    flux_right, reach_right = side_flux(right_state, face_speed, normal)
    reach = jnp.maximum(reach_left, reach_right)
    return 0.5 * (flux_left + flux_right) - 0.5 * reach[:, None] * (right_state - left_state)


def section_update(flow, grid_velocity, cell_volume, ext_state, ext_grid, derivative):
    flux_x = face_flux(
        ext_state[:, :, :-1], ext_state[:, :, 1:], ext_grid[:, :, :-1], ext_grid[:, :, 1:], 0
    )
    state_y = jnp.concatenate([flow[..., :1], flow, flow[..., -1:]], axis=3)
    grid_y = jnp.concatenate(
        [grid_velocity[..., :1], grid_velocity, grid_velocity[..., -1:]], axis=3
    )
    flux_y = face_flux(state_y[..., :-1], state_y[..., 1:], grid_y[..., :-1], grid_y[..., 1:], 1)
    divergence = (
        flux_x[:, :, 1:] - flux_x[:, :, :-1] + flux_y[..., 1:] - flux_y[..., :-1]
    ) / cell_volume
    residual = derivative + divergence
    velocity, pressure, sound = cell_state(flow)
    reach_sum = (
        jnp.abs(velocity[:, 0] - grid_velocity[:, 0])
        + jnp.abs(velocity[:, 1] - grid_velocity[:, 1])
        + 2.0 * sound
    )
    pseudo_step = courant_number * cell_volume / (reach_sum + math.pi * cell_volume)
    return flow - section_weight * pseudo_step[:, None] * residual


def body(flow, grid_velocity, cell_volume):
    inst_count = lax.axis_size("inst")
    own_index = lax.axis_index("inst")
    packed = jnp.concatenate([flow, grid_velocity], axis=1)
    extended = extended_2(packed, (("space", 2),), 1)
    ext_state = extended[:, :5]
    ext_grid = extended[:, 5:]
    slices = lax.all_gather(flow, "inst", axis=0, tiled=True)
    positions = jnp.arange(slices.shape[0], dtype=jnp.int32)
    weights = coefficient((own_index - positions) % inst_count, inst_count)
    added = jnp.einsum("j,jvxy->vxy", weights, slices, precision=lax.Precision.HIGHEST)
    derivative = added[None]
    summed = jnp.sum(slices, axis=0, keepdims=True)
    slab_width = flow.shape[3] // inst_count
    mean_flow = (
        lax.dynamic_slice_in_dim(summed[0], own_index * slab_width, slab_width, 2) / inst_count
    )
    flow_next = section_update(flow, grid_velocity, cell_volume, ext_state, ext_grid, derivative)
    return (flow_next, mean_flow)


def solution(mesh):
    in_specs = (
        P(("groups", "inst"), None, "space", None),
        P(("groups", "inst"), None, "space", None),
        P("space", None),
    )
    out_specs = (P(("groups", "inst"), None, "space", None), P("groups", "space", "inst"))
    return jax.shard_map(body, mesh=mesh, in_specs=in_specs, out_specs=out_specs, check_vma=False)
```

profile of v0, /device:TPU:0, one launch (start us, length us, event | category | flops | bytes accessed | tf_op | source)
XLA Modules:
  0.0 121.0 jit_solution(16029202322969365689)
XLA Ops:
  7.2 0.7 all-gather.2.cloned.1.call-update
  7.9 1.2 constant_dynamic-update-slice_fusion.1
  9.2 0.5 collective-permute-start
  9.7 0.1 collective-permute-start.1
  9.9 0.1 fusion.87
  10.0 0.1 fusion.76
  10.2 0.3 multiply_reduce_fusion.3
  10.5 0.1 fusion.41
  10.6 0.1 multiply_bitcast_fusion.9
  10.7 0.2 multiply_bitcast_fusion.7
  10.9 0.4 copy-done.3
  11.4 0.5 multiply_subtract_fusion.1
  11.8 0.4 copy-done.2
  12.3 0.1 fusion.33
  12.5 0.2 multiply_reduce_fusion.1
  12.7 0.1 fusion.39
  12.8 0.2 multiply_bitcast_fusion.2
  13.0 0.4 copy-done.5
  13.4 0.5 multiply_subtract_fusion
  14.0 85.2 %all-gather.2.cloned.1.call-done = f32[8,5,32,1024]{3,2,1,0:T(8,128)} async-done(((f32[1,5,32,1024]{3,2,1,0:T(8,128)}), f32[8,5,32,1024]{3,2,1,0:T(8,128)}) %all-gather.2.cloned.1.call-update) | async-done | bytes 5242896 | tf_op jit(solution)/shard_map/all_gather | solution.py:96
  99.2 3.1 %reduce_sum.59 = f32[5,32,1024]{2,1,0:T(8,128)S(1)} reduce(f32[8,5,32,1024]{3,2,1,0:T(8,128)} %all-gather.2.cloned.1.call-done, f32[]{:T(128)} %constant.28.clone.1), dimensions={0}, to_apply=%region_5.6 | reduce | flops 1146880 | bytes 5898244 | tf_op jit(solution)/shard_map/reduce_sum | solution.py:101
  102.3 0.7 dynamic-slice_multiply_fusion
  102.9 9.9 %fusion = f32[1,5,32,1024]{3,0,2,1:T(1,128)S(1)} fusion(f32[8,5,32,1024]{3,2,1,0:T(8,128)} %all-gather.2.cloned.1.call-done, s32[]{:T(128)S(6)} %axis_index.15), kind=kOutput, calls=%fused_computation | convolution fusion | flops 15728912 | bytes 5898244 | tf_op jit(solution)/shard_map/j,jvxy->vxy/dot_general | solution.py:99
  112.8 1.3 %fusion.7 = f32[1,5,32,1024]{3,2,1,0:T(8,128)} fusion(f32[1,5,32,1024]{3,2,1,0:T(8,128)S(1)} %copy-done, f32[1,5,32,1025]{3,2,1,0:T(8,128)S(1)} %multiply_subtract_fusion.1, f32[1,5,33,1024]{3,2,1,0:T(8,128)S(1)} %multiply_subtract_fusion, f32[1,5,32,1024]{3,0,2,1:T(1,128)S(1)} %fusion, f32[32,1024]{1,0:T(8,128)S(1)} %copy-done.2, f32[32,1024]{1,0:T(8,128)S(1)} %fusion.33), kind=kLoop, calls=%fused_computation.38 | loop fusion | flops 1146880 | bytes 4849664 | tf_op jit(solution)/shard_map/sub | solution.py:86
  (18 shorter events, 0.3 us)
Async XLA Ops:
  7.2 2.0 %copy-start.1 = (f32[1,2,32,1024]{3,2,1,0:T(8,128)S(1)}, f32[1,2,32,1024]{3,2,1,0:T(8,128)}, u32[]{:S(2)}) copy-start(f32[1,2,32,1024]{3,2,1,0:T(8,128)} %param.12) | copy-start | bytes 786436
  7.2 92.0 %all-gather.2.cloned.1.call-start = ((), (), s32[]{:S(2)}) async-start(), calls=%async_computation | async-start | bytes 5898240 | tf_op jit(solution)/shard_map/all_gather | solution.py:96
  7.9 2.0 %copy-start = (f32[1,5,32,1024]{3,2,1,0:T(8,128)S(1)}, f32[1,5,32,1024]{3,2,1,0:T(8,128)}, u32[]{:S(2)}) copy-start(f32[1,5,32,1024]{3,2,1,0:T(8,128)} %param.11) | copy-start | bytes 1966084
  9.2 3.2 %collective-permute-start = (f32[1,7,1,1024]{3,2,1,0:T(1,128)S(1)}, f32[1,7,1,1024]{3,2,1,0:T(1,128)S(1)}, u32[]{:S(2)}, u32[]{:S(2)}) collective-permute-start(f32[1,7,1,1024]{3,2,1,0:T(1,128)S(1)} %get-tuple-element.30), channel_id=1, source_target_pairs={{0,1},{1,0},{2,3},{3,2},{4,5},{5,4},{6,7},{7,6},{8,9},{9,8},{10,11... | collective-permute-start | bytes 86024 | tf_op jit(solution)/shard_map/ppermute | solution.py:21
  9.7 2.7 %collective-permute-start.1 = (f32[1,7,1,1024]{3,2,1,0:T(1,128)S(1)}, f32[1,7,1,1024]{3,2,1,0:T(1,128)S(1)}, u32[]{:S(2)}, u32[]{:S(2)}) collective-permute-start(f32[1,7,1,1024]{3,2,1,0:T(1,128)S(1)} %get-tuple-element.31), channel_id=1, source_target_pairs={{1,0},{0,1},{3,2},{2,3},{5,4},{4,5},{7,6},{6,7},{9,8},{8,9},{11,10... | collective-permute-start | bytes 86024 | tf_op jit(solution)/shard_map/ppermute | solution.py:22
  10.7 0.7 copy-start.3
  10.7 0.7 copy-start.4
  11.4 0.9 copy-start.2
  12.8 0.7 copy-start.5
Sparse Core Ops, SparseCore 0:
  10.2 88.9 all-gather.1
where the time goes:
time: 121 us
  waiting for transfers between devices  85.9 us (71%)
  between operations  14.2 us (12%)
  matrix products  9.9 us (8%)
  other arithmetic  7.49 us (6%)
  local copies, waits for them, and re-layouts  2.8 us (2%)
    all_gather x1, waiting for transfers between devices, body(): slices = lax.all_gather(flow, 'inst', axis=0, tiled=True)  85.2 us
    dot_general x1, matrix products, body(): jnp.einsum('j,jvxy->vxy', weights, slices, precision=lax.Precision.HIGHEST)  9.9 us
    reduce_sum x1, other arithmetic, body(): summed = jnp.sum(slices, axis=0, keepdims=True)  3.07 us
    unnamed x13, local copies, waits for them, and re-layouts  2.57 us
  transfers between devices with their start and end apart: 3, of which 1 were waited for; matrix products, arithmetic and copies ran while one was open for 3% of the time, Pallas kernels for 0%

commit v1 on v0

--- a/solution.py
+++ b/solution.py
@@ -1,9 +1,12 @@
+import functools
 import math
 
 import jax
 import jax.numpy as jnp
 import numpy as np
 from jax import lax
+from jax.experimental import pallas as pl
+from jax.experimental.pallas import tpu as pltpu
 from jax.sharding import PartitionSpec as P
 
 gamma_ratio = 1.4
@@ -107,6 +110,238 @@
     return (flow_next, mean_flow)
 
 
+LANES = 128
+
+
+def spectral_weight(offset, count):
+    if offset == 0:
+        return 0.0
+    angle = math.pi * offset / count
+    return (-1.0) ** offset * (math.pi / count) * math.cos(angle) / math.sin(angle)
+
+
+def cell_terms(state):
+    inverse = 1.0 / state[0]
+    speeds = [state[k] * inverse for k in (1, 2, 3)]
+    kinetic = 0.5 * (state[1] * speeds[0] + state[2] * speeds[1] + state[3] * speeds[2])
+    pressure = (gamma_ratio - 1.0) * (state[4] - kinetic)
+    sound = jnp.sqrt(gamma_ratio * pressure * inverse)
+    return speeds[0], speeds[1], pressure, sound
+
+
+def rusanov(left, right, normal):
+    state_l, speed_l, pressure_l, sound_l, grid_l = left
+    state_r, speed_r, pressure_r, sound_r, grid_r = right
+    face_speed = 0.5 * (grid_l + grid_r)
+    relative_l = speed_l - face_speed
+    relative_r = speed_r - face_speed
+    reach = jnp.maximum(jnp.abs(relative_l) + sound_l, jnp.abs(relative_r) + sound_r)
+    weight_l = 0.5 * (relative_l + reach)
+    weight_r = 0.5 * (relative_r - reach)
+    flux = [a * weight_l + b * weight_r for a, b in zip(state_l, state_r)]
+    flux[1 + normal] += 0.5 * (pressure_l + pressure_r)
+    flux[4] += 0.5 * (pressure_l * speed_l + pressure_r * speed_r)
+    return flux
+
+
+def on_side(change, side):
+    return ([change(x) for x in side[0]],) + tuple(change(x) for x in side[1:])
+
+
+def section_kernel(
+    n,
+    flow_ref,
+    grid_ref,
+    volume_ref,
+    next_ref,
+    mean_ref,
+    slabs,
+    rates,
+    returned,
+    step_ref,
+    edge_out,
+    edge_in,
+    edge_send,
+    edge_recv,
+    slab_send,
+    slab_recv,
+    rate_send,
+    rate_recv,
+):
+    variables, rows, columns = flow_ref.shape
+    width = columns // n
+    me = lax.axis_index("inst")
+    other = 1 - lax.axis_index("space")
+    order = sorted(range(1, n), key=lambda s: abs(2 * s - n))
+
+    def peer(offset):
+        return lax.rem(me + (offset + n), n)
+
+    def columns_of(offset):
+        return pl.ds(pl.multiple_of(peer(offset) * width, width), width)
+
+    barrier = pltpu.get_barrier_semaphore()
+    for s in range(1, n):
+        pl.semaphore_signal(barrier, inc=1, device_id={"inst": peer(s)})
+    pl.semaphore_signal(barrier, inc=1, device_id={"space": other})
+    for edge, row in ((0, rows - 1), (1, 0)):
+        for v in range(variables):
+            edge_out[edge, v : v + 1, :] = flow_ref[v, row : row + 1, :]
+        for v in range(2):
+            edge_out[edge, variables + v : variables + v + 1, :] = grid_ref[v, row : row + 1, :]
+        edge_out[edge, variables + 2 : variables + 3, :] = jnp.zeros((1, columns), jnp.float32)
+    pl.semaphore_wait(barrier, n)
+
+    edges = pltpu.make_async_remote_copy(
+        src_ref=edge_out,
+        dst_ref=edge_in,
+        send_sem=edge_send,
+        recv_sem=edge_recv,
+        device_id={"space": other},
+    )
+    edges.start()
+    for c in range(variables):
+        for s in order:
+            pltpu.make_async_remote_copy(
+                src_ref=flow_ref.at[c, :, columns_of(s)],
+                dst_ref=slabs.at[c, s - 1],
+                send_sem=slab_send,
+                recv_sem=slab_recv.at[c],
+                device_id={"inst": peer(s)},
+            ).start()
+
+    state = [flow_ref[v] for v in range(variables)]
+    grid_0, grid_1, volume = grid_ref[0], grid_ref[1], volume_ref[...]
+    speed_0, speed_1, pressure, sound = cell_terms(state)
+    wave = jnp.abs(speed_0 - grid_0) + jnp.abs(speed_1 - grid_1) + 2.0 * sound
+    push = (section_weight * courant_number) / (wave + math.pi * volume)
+    step_ref[...] = push * volume
+
+    lane = lax.broadcasted_iota(jnp.int32, (rows, columns), 1)
+    own = (state, speed_1, pressure, sound, grid_1)
+    left = on_side(lambda x: jnp.where(lane == 0, x, pltpu.roll(x, 1, 1)), own)
+    flux = rusanov(left, own, 1)
+    end = on_side(lambda x: x[:, columns - LANES :], own)
+    last = rusanov(end, end, 1)
+    lane_end = lane[:, columns - LANES :]
+    for v in range(variables):
+        upper = pltpu.roll(flux[v], columns - 1, 1)
+        upper_end = jnp.where(lane_end == columns - 1, last[v], upper[:, columns - LANES :])
+        upper = jnp.concatenate([upper[:, : columns - LANES], upper_end], axis=1)
+        next_ref[v] = state[v] - push * (upper - flux[v])
+
+    edges.wait_recv()
+
+    def edge_side(edge):
+        edge_state = [edge_in[edge, v : v + 1, :] for v in range(variables)]
+        speed, _, edge_pressure, edge_sound = cell_terms(edge_state)
+        grid = edge_in[edge, variables : variables + 1, :]
+        return (edge_state, speed, edge_pressure, edge_sound, grid)
+
+    above, below = edge_side(0), edge_side(1)
+    row = lax.broadcasted_iota(jnp.int32, (rows, columns), 0)
+    own = (state, speed_0, pressure, sound, grid_0)
+    rolled = on_side(lambda x: pltpu.roll(x, 1, 0), own)
+    first = lambda x, y: jnp.where(row == 0, y, x)
+    left = (
+        [first(x, y) for x, y in zip(rolled[0], above[0])],
+    ) + tuple(first(x, y) for x, y in zip(rolled[1:], above[1:]))
+    flux = rusanov(left, own, 0)
+    last = rusanov(on_side(lambda x: x[rows - 1 : rows], own), below, 0)
+    for v in range(variables):
+        upper = jnp.where(row == rows - 1, last[v], pltpu.roll(flux[v], rows - 1, 0))
+        next_ref[v] = next_ref[v] - push * (upper - flux[v])
+
+    for c in range(variables):
+        got = slabs.at[c]
+        pltpu.make_async_remote_copy(
+            src_ref=got,
+            dst_ref=got,
+            send_sem=slab_send,
+            recv_sem=slab_recv.at[c],
+            device_id={"inst": peer(1)},
+        ).wait_recv()
+        held = [flow_ref[c, :, columns_of(0)]] + [slabs[c, s - 1] for s in range(1, n)]
+        mean_ref[c] = functools.reduce(jnp.add, held) * (1.0 / n)
+
+        def rate(t):
+            terms = [held[s] * spectral_weight((s - t) % n, n) for s in range(n) if s != t]
+            return functools.reduce(jnp.add, terms)
+
+        for t in order:
+            rates[c, t - 1] = rate(t)
+            pltpu.make_async_remote_copy(
+                src_ref=rates.at[c, t - 1],
+                dst_ref=returned.at[c, t - 1],
+                send_sem=rate_send,
+                recv_sem=rate_recv.at[c],
+                device_id={"inst": peer(-t)},
+            ).start()
+        at = columns_of(0)
+        next_ref[c, :, at] = next_ref[c, :, at] - step_ref[:, at] * rate(0)
+
+    for c in range(variables):
+        got = returned.at[c]
+        pltpu.make_async_remote_copy(
+            src_ref=got,
+            dst_ref=got,
+            send_sem=rate_send,
+            recv_sem=rate_recv.at[c],
+            device_id={"inst": peer(1)},
+        ).wait_recv()
+        for t in range(1, n):
+            at = columns_of(t)
+            next_ref[c, :, at] = next_ref[c, :, at] - step_ref[:, at] * returned[c, t - 1]
+
+    edges.wait_send()
+    for sent, sem in ((slabs, slab_send), (rates, rate_send)):
+        pltpu.make_async_remote_copy(
+            src_ref=sent,
+            dst_ref=sent,
+            send_sem=sem,
+            recv_sem=edge_recv,
+            device_id={"inst": peer(1)},
+        ).wait_send()
+
+
+def kernel_body(flow, grid_velocity, cell_volume):
+    n = lax.axis_size("inst")
+    variables, rows, columns = flow.shape[1:]
+    width = columns // n
+    f32 = jnp.float32
+    exchanged = pltpu.VMEM((variables, n - 1, rows, width), f32)
+    edge = pltpu.VMEM((2, variables + 3, columns), f32)
+    dma = pltpu.SemaphoreType.DMA
+    flow_next, mean_flow = pl.pallas_call(
+        functools.partial(section_kernel, n),
+        out_shape=(
+            jax.ShapeDtypeStruct((variables, rows, columns), f32),
+            jax.ShapeDtypeStruct((variables, rows, width), f32),
+        ),
+        in_specs=[pl.BlockSpec(memory_space=pltpu.VMEM)] * 3,
+        out_specs=[pl.BlockSpec(memory_space=pltpu.VMEM)] * 2,
+        scratch_shapes=[
+            exchanged,
+            exchanged,
+            exchanged,
+            pltpu.VMEM((rows, columns), f32),
+            edge,
+            edge,
+            dma,
+            dma,
+            dma,
+            dma((variables,)),
+            dma,
+            dma((variables,)),
+        ],
+        compiler_params=pltpu.CompilerParams(
+            collective_id=0, has_side_effects=True, vmem_limit_bytes=32 * 1024 * 1024
+        ),
+        name="section",
+    )(flow[0], grid_velocity[0], cell_volume)
+    return flow_next[None], mean_flow
+
+
 def solution(mesh):
     in_specs = (
         P(("groups", "inst"), None, "space", None),
@@ -114,4 +349,12 @@
         P("space", None),
     )
     out_specs = (P(("groups", "inst"), None, "space", None), P("groups", "space", "inst"))
-    return jax.shard_map(body, mesh=mesh, in_specs=in_specs, out_specs=out_specs, check_vma=False)
+
+    def local(flow, grid_velocity, cell_volume):
+        whole_lanes = flow.shape[3] % (LANES * mesh.shape["inst"]) == 0
+        whole_rows = flow.shape[2] % 8 == 0 and flow.shape[2] >= 8
+        fits = mesh.shape["space"] == 2 and mesh.shape["inst"] > 1 and flow.shape[0] == 1
+        chosen = kernel_body if whole_lanes and whole_rows and fits else body
+        return chosen(flow, grid_velocity, cell_volume)
+
+    return jax.shard_map(local, mesh=mesh, in_specs=in_specs, out_specs=out_specs, check_vma=False)

time: 121 us -> 40.3 us (0.33)
  waiting for transfers between devices: 85.9 us -> 0 us
  Pallas kernels: 0 us -> 35.1 us
  between operations: 14.2 us -> 0.65 us
  matrix products: 9.9 us -> 0 us
  other arithmetic: 7.49 us -> 0 us
  local copies, waits for them, and re-layouts: 2.8 us -> 4.41 us
    all_gather x1 -> x0, waiting for transfers between devices: 85.2 us -> none  [body(): slices = lax.all_gather(flow, 'inst', axis=0, tiled=True)]
    pallas_call x0 -> x1, Pallas kernels: none -> 35.1 us  [kernel_body(): pl.pallas_call(functools.partial(section_kernel, n), out_shape=(jax.Shape...]
    dot_general x1 -> x0, matrix products: 9.9 us -> none  [body(): jnp.einsum('j,jvxy->vxy', weights, slices, precision=lax.Precision.HIGHEST)]
    reduce_sum x4 -> x0, other arithmetic: 3.63 us -> none  [the longest x1 3.07 us: body(): summed = jnp.sum(slices, axis=0, keepdims=True)]
    sub x3 -> x0, other arithmetic: 2.25 us -> none  [the longest x1 1.29 us: section_update(): return flow - section_weight * pseudo_step[:, None] * residual]
    unnamed x13 -> x8, local copies, waits for them, and re-layouts: 2.57 us -> 4.41 us
  transfers between devices with their start and end apart: 3 -> 0, of which waited for: 1 -> 0; matrix products, arithmetic and copies ran while one was open for 3% -> 0% of each run, Pallas kernels for 0% -> 0%
where the time goes in v1:
time: 40.3 us; the launch traced here: 40.1 us
  Pallas kernels  35.1 us (87%)
  local copies, waits for them, and re-layouts  4.41 us (11%)
  between operations  0.65 us (2%)
    pallas_call x1, Pallas kernels, kernel_body(): pl.pallas_call(functools.partial(section_kernel, n), out_shape=(jax.Shape...  35.1 us
    unnamed x8, local copies, waits for them, and re-layouts  4.41 us

profile of v1, /device:TPU:0, one launch (start us, length us, event | category | flops | bytes accessed | tf_op | source)
XLA Modules:
  0.0 40.1 jit_solution(2114894677989214697)
XLA Ops:
  0.6 0.0 copy-start
  0.6 1.1 %copy-done = f32[1,5,32,1024]{3,2,1,0:T(8,128)S(1)} copy-done((f32[1,5,32,1024]{3,2,1,0:T(8,128)S(1)}, f32[1,5,32,1024]{3,2,1,0:T(8,128)}, u32[]{:S(2)}) %copy-start) | copy-done | bytes 655384
  1.7 0.0 copy-start.1
  1.7 0.9 %copy-done.1 = f32[1,2,32,1024]{3,2,1,0:T(8,128)S(1)} copy-done((f32[1,2,32,1024]{3,2,1,0:T(8,128)S(1)}, f32[1,2,32,1024]{3,2,1,0:T(8,128)}, u32[]{:S(2)}) %copy-start.1) | copy-done | bytes 262168
  2.7 0.0 copy-start.2
  2.7 0.9 %copy-done.2 = f32[32,1024]{1,0:T(8,128)S(1)} copy-done((f32[32,1024]{1,0:T(8,128)S(1)}, f32[32,1024]{1,0:T(8,128)}, u32[]{:S(2)}) %copy-start.2) | copy-done | bytes 131096
  3.6 35.1 %section.1 = (f32[5,32,1024]{2,1,0:T(8,128)S(1)}, f32[5,32,128]{2,1,0:T(8,128)S(1)}) custom-call(f32[5,32,1024]{2,1,0:T(8,128)S(1)} %bitcast.4, f32[2,32,1024]{2,1,0:T(8,128)S(1)} %bitcast.5, f32[32,1024]{1,0:T(8,128)S(1)} %copy-done.2), custom_call_target="tpu_custom_call" | custom-call | tf_op jit(solution)/shard_map/section/pallas_call | solution.py:315
  38.6 0.8 %copy.7 = f32[1,5,32,1024]{3,2,1,0:T(8,128)} copy(f32[1,5,32,1024]{3,2,1,0:T(8,128)S(1)} %bitcast.3) | data formatting | bytes 1310720
  39.5 0.6 %copy.8 = f32[5,32,128]{2,1,0:T(8,128)} copy(f32[5,32,128]{2,1,0:T(8,128)S(1)} %get-tuple-element.9) | data formatting | bytes 163840
Async XLA Ops:
  0.6 1.1 %copy-start = (f32[1,5,32,1024]{3,2,1,0:T(8,128)S(1)}, f32[1,5,32,1024]{3,2,1,0:T(8,128)}, u32[]{:S(2)}) copy-start(f32[1,5,32,1024]{3,2,1,0:T(8,128)} %param.3) | copy-start | bytes 1966084
  1.7 0.9 %copy-start.1 = (f32[1,2,32,1024]{3,2,1,0:T(8,128)S(1)}, f32[1,2,32,1024]{3,2,1,0:T(8,128)}, u32[]{:S(2)}) copy-start(f32[1,2,32,1024]{3,2,1,0:T(8,128)} %param.4) | copy-start | bytes 786436
  2.7 0.9 %copy-start.2 = (f32[32,1024]{1,0:T(8,128)S(1)}, f32[32,1024]{1,0:T(8,128)}, u32[]{:S(2)}) copy-start(f32[32,1024]{1,0:T(8,128)} %volume_ref.1) | copy-start | bytes 393220

commit v2 on v1

--- a/solution.py
+++ b/solution.py
@@ -150,11 +150,14 @@
 
 def section_kernel(
     n,
+    flow_hbm,
+    grid_hbm,
+    volume_hbm,
+    next_ref,
+    mean_ref,
     flow_ref,
     grid_ref,
     volume_ref,
-    next_ref,
-    mean_ref,
     slabs,
     rates,
     returned,
@@ -167,6 +170,7 @@
     slab_recv,
     rate_send,
     rate_recv,
+    load_sem,
 ):
     variables, rows, columns = flow_ref.shape
     width = columns // n
@@ -180,10 +184,20 @@
     def columns_of(offset):
         return pl.ds(pl.multiple_of(peer(offset) * width, width), width)
 
+    loads = [
+        pltpu.make_async_copy(source, target, load_sem.at[k])
+        for k, (source, target) in enumerate(
+            ((flow_hbm, flow_ref), (grid_hbm, grid_ref), (volume_hbm, volume_ref))
+        )
+    ]
+    for load in loads:
+        load.start()
     barrier = pltpu.get_barrier_semaphore()
     for s in range(1, n):
         pl.semaphore_signal(barrier, inc=1, device_id={"inst": peer(s)})
     pl.semaphore_signal(barrier, inc=1, device_id={"space": other})
+    for load in loads:
+        load.wait()
     for edge, row in ((0, rows - 1), (1, 0)):
         for v in range(variables):
             edge_out[edge, v : v + 1, :] = flow_ref[v, row : row + 1, :]
@@ -318,9 +332,12 @@
             jax.ShapeDtypeStruct((variables, rows, columns), f32),
             jax.ShapeDtypeStruct((variables, rows, width), f32),
         ),
-        in_specs=[pl.BlockSpec(memory_space=pltpu.VMEM)] * 3,
+        in_specs=[pl.BlockSpec(memory_space=pltpu.HBM)] * 3,
         out_specs=[pl.BlockSpec(memory_space=pltpu.VMEM)] * 2,
         scratch_shapes=[
+            pltpu.VMEM((variables, rows, columns), f32),
+            pltpu.VMEM((2, rows, columns), f32),
+            pltpu.VMEM((rows, columns), f32),
             exchanged,
             exchanged,
             exchanged,
@@ -333,12 +350,13 @@
             dma((variables,)),
             dma,
             dma((variables,)),
+            dma((3,)),
         ],
         compiler_params=pltpu.CompilerParams(
             collective_id=0, has_side_effects=True, vmem_limit_bytes=32 * 1024 * 1024
         ),
         name="section",
-    )(flow[0], grid_velocity[0], cell_volume)
+    )(*[pltpu.with_memory_space_constraint(x, pltpu.HBM) for x in (flow[0], grid_velocity[0], cell_volume)])
     return flow_next[None], mean_flow
 
 

time: 40.3 us -> 37.4 us (0.928)
  local copies, waits for them, and re-layouts: 4.41 us -> 1.47 us
    unnamed x8 -> x2, local copies, waits for them, and re-layouts: 4.41 us -> 1.47 us
where the time goes in v2:
time: 37.4 us; the launch traced here: 37.3 us
  Pallas kernels  35.2 us (94%)
  local copies, waits for them, and re-layouts  1.47 us (4%)
  between operations  0.64 us (2%)
    pallas_call x1, Pallas kernels, kernel_body(): pl.pallas_call(functools.partial(section_kernel, n), out_shape=(jax.Shape...  35.2 us
    unnamed x2, local copies, waits for them, and re-layouts  1.47 us

profile of v2, /device:TPU:0, one launch (start us, length us, event | category | flops | bytes accessed | tf_op | source)
XLA Modules:
  0.0 37.3 jit_solution(8586282590373701843)
XLA Ops:
  0.6 35.2 %section.1 = (f32[5,32,1024]{2,1,0:T(8,128)S(1)}, f32[5,32,128]{2,1,0:T(8,128)S(1)}) custom-call(f32[5,32,1024]{2,1,0:T(8,128)} %bitcast.4, f32[2,32,1024]{2,1,0:T(8,128)} %bitcast.5, f32[32,1024]{1,0:T(8,128)} %volume_hbm.1), custom_call_target="tpu_custom_call" | custom-call | tf_op jit(solution)/shard_map/section/pallas_call | solution.py:329
  35.8 0.8 %copy.7 = f32[1,5,32,1024]{3,2,1,0:T(8,128)} copy(f32[1,5,32,1024]{3,2,1,0:T(8,128)S(1)} %bitcast.3) | data formatting | bytes 1310720
  36.6 0.6 %copy.8 = f32[5,32,128]{2,1,0:T(8,128)} copy(f32[5,32,128]{2,1,0:T(8,128)S(1)} %get-tuple-element.9) | data formatting | bytes 163840

commit v3 on v2

--- a/solution.py
+++ b/solution.py
@@ -318,6 +318,17 @@
         ).wait_send()
 
 
+def write_kernel(next_ref, mean_ref, next_hbm, mean_hbm, sems):
+    writes = [
+        pltpu.make_async_copy(next_ref, next_hbm, sems.at[0]),
+        pltpu.make_async_copy(mean_ref, mean_hbm, sems.at[1]),
+    ]
+    for write in writes:
+        write.start()
+    for write in writes:
+        write.wait()
+
+
 def kernel_body(flow, grid_velocity, cell_volume):
     n = lax.axis_size("inst")
     variables, rows, columns = flow.shape[1:]
@@ -329,8 +340,8 @@
     flow_next, mean_flow = pl.pallas_call(
         functools.partial(section_kernel, n),
         out_shape=(
-            jax.ShapeDtypeStruct((variables, rows, columns), f32),
-            jax.ShapeDtypeStruct((variables, rows, width), f32),
+            pltpu.VMEM((variables, rows, columns), f32),
+            pltpu.VMEM((variables, rows, width), f32),
         ),
         in_specs=[pl.BlockSpec(memory_space=pltpu.HBM)] * 3,
         out_specs=[pl.BlockSpec(memory_space=pltpu.VMEM)] * 2,
@@ -357,6 +368,17 @@
         ),
         name="section",
     )(*[pltpu.with_memory_space_constraint(x, pltpu.HBM) for x in (flow[0], grid_velocity[0], cell_volume)])
+    flow_next, mean_flow = pl.pallas_call(
+        write_kernel,
+        out_shape=(
+            jax.ShapeDtypeStruct(flow_next.shape, f32),
+            jax.ShapeDtypeStruct(mean_flow.shape, f32),
+        ),
+        in_specs=[pl.BlockSpec(memory_space=pltpu.VMEM)] * 2,
+        out_specs=[pl.BlockSpec(memory_space=pltpu.HBM)] * 2,
+        scratch_shapes=[dma((2,))],
+        name="write",
+    )(*[pltpu.with_memory_space_constraint(x, pltpu.VMEM) for x in (flow_next, mean_flow)])
     return flow_next[None], mean_flow
 
 

time: 37.4 us -> 36.8 us (0.984)
  local copies, waits for them, and re-layouts: 1.47 us -> 0 us
  Pallas kernels: 35.2 us -> 36 us
    unnamed x2 -> x0, local copies, waits for them, and re-layouts: 1.47 us -> none
    pallas_call x1 -> x2, Pallas kernels: 35.2 us -> 36 us  [the longest x1 35.2 us: kernel_body(): pl.pallas_call(functools.partial(section_kernel, n), out_shape=(pltpu.VME...]
where the time goes in v3:
time: 36.8 us; the launch traced here: 36.7 us
  Pallas kernels  36 us (98%)
  between operations  0.64 us (2%)
    pallas_call x1, Pallas kernels, kernel_body(): pl.pallas_call(functools.partial(section_kernel, n), out_shape=(pltpu.VME...  35.2 us
    pallas_call x1, Pallas kernels, kernel_body(): pl.pallas_call(write_kernel, out_shape=(jax.ShapeDtypeStruct(flow_next.sh...  0.87 us

profile of v3, /device:TPU:0, one launch (start us, length us, event | category | flops | bytes accessed | tf_op | source)
XLA Modules:
  0.0 36.7 jit_solution(13842771530694217879)
XLA Ops:
  0.6 35.2 %section.1 = (f32[5,32,1024]{2,1,0:T(8,128)S(1)}, f32[5,32,128]{2,1,0:T(8,128)S(1)}) custom-call(f32[5,32,1024]{2,1,0:T(8,128)} %bitcast.3, f32[2,32,1024]{2,1,0:T(8,128)} %bitcast.4, f32[32,1024]{1,0:T(8,128)} %volume_hbm.1), custom_call_target="tpu_custom_call" | custom-call | tf_op jit(solution)/shard_map/section/pallas_call | solution.py:340
  35.8 0.9 %write.1 = (f32[5,32,1024]{2,1,0:T(8,128)}, f32[5,32,128]{2,1,0:T(8,128)}) custom-call(f32[5,32,1024]{2,1,0:T(8,128)S(1)} %get-tuple-element.6.next_ref, f32[5,32,128]{2,1,0:T(8,128)S(1)} %get-tuple-element.7.mean_ref), custom_call_target="tpu_custom_call" | custom-call | tf_op jit(solution)/shard_map/write/pallas_call | solution.py:371

commit v4 on v3

--- a/solution.py
+++ b/solution.py
@@ -111,6 +111,7 @@
 
 
 LANES = 128
+PIECES = 2
 
 
 def spectral_weight(offset, count):
@@ -214,13 +215,15 @@
         device_id={"space": other},
     )
     edges.start()
-    for c in range(variables):
+    cuts = [-(-variables * k // PIECES) for k in range(PIECES + 1)]
+    pieces = list(enumerate(slice(a, b) for a, b in zip(cuts, cuts[1:])))
+    for k, c in pieces:
         for s in order:
             pltpu.make_async_remote_copy(
                 src_ref=flow_ref.at[c, :, columns_of(s)],
-                dst_ref=slabs.at[c, s - 1],
+                dst_ref=slabs.at[s - 1, c],
                 send_sem=slab_send,
-                recv_sem=slab_recv.at[c],
+                recv_sem=slab_recv.at[k],
                 device_id={"inst": peer(s)},
             ).start()
 
@@ -266,16 +269,16 @@
         upper = jnp.where(row == rows - 1, last[v], pltpu.roll(flux[v], rows - 1, 0))
         next_ref[v] = next_ref[v] - push * (upper - flux[v])
 
-    for c in range(variables):
-        got = slabs.at[c]
+    for k, c in pieces:
+        got = slabs.at[:, c]
         pltpu.make_async_remote_copy(
             src_ref=got,
             dst_ref=got,
             send_sem=slab_send,
-            recv_sem=slab_recv.at[c],
+            recv_sem=slab_recv.at[k],
             device_id={"inst": peer(1)},
         ).wait_recv()
-        held = [flow_ref[c, :, columns_of(0)]] + [slabs[c, s - 1] for s in range(1, n)]
+        held = [flow_ref[c, :, columns_of(0)]] + [slabs[s - 1, c] for s in range(1, n)]
         mean_ref[c] = functools.reduce(jnp.add, held) * (1.0 / n)
 
         def rate(t):
@@ -283,29 +286,29 @@
             return functools.reduce(jnp.add, terms)
 
         for t in order:
-            rates[c, t - 1] = rate(t)
+            rates[t - 1, c] = rate(t)
             pltpu.make_async_remote_copy(
-                src_ref=rates.at[c, t - 1],
-                dst_ref=returned.at[c, t - 1],
+                src_ref=rates.at[t - 1, c],
+                dst_ref=returned.at[t - 1, c],
                 send_sem=rate_send,
-                recv_sem=rate_recv.at[c],
+                recv_sem=rate_recv.at[k],
                 device_id={"inst": peer(-t)},
             ).start()
         at = columns_of(0)
         next_ref[c, :, at] = next_ref[c, :, at] - step_ref[:, at] * rate(0)
 
-    for c in range(variables):
-        got = returned.at[c]
+    for k, c in pieces:
+        got = returned.at[:, c]
         pltpu.make_async_remote_copy(
             src_ref=got,
             dst_ref=got,
             send_sem=rate_send,
-            recv_sem=rate_recv.at[c],
+            recv_sem=rate_recv.at[k],
             device_id={"inst": peer(1)},
         ).wait_recv()
         for t in range(1, n):
             at = columns_of(t)
-            next_ref[c, :, at] = next_ref[c, :, at] - step_ref[:, at] * returned[c, t - 1]
+            next_ref[c, :, at] = next_ref[c, :, at] - step_ref[:, at] * returned[t - 1, c]
 
     edges.wait_send()
     for sent, sem in ((slabs, slab_send), (rates, rate_send)):
@@ -334,7 +337,7 @@
     variables, rows, columns = flow.shape[1:]
     width = columns // n
     f32 = jnp.float32
-    exchanged = pltpu.VMEM((variables, n - 1, rows, width), f32)
+    exchanged = pltpu.VMEM((n - 1, variables, rows, width), f32)
     edge = pltpu.VMEM((2, variables + 3, columns), f32)
     dma = pltpu.SemaphoreType.DMA
     flow_next, mean_flow = pl.pallas_call(
@@ -358,9 +361,9 @@
             dma,
             dma,
             dma,
-            dma((variables,)),
+            dma((PIECES,)),
             dma,
-            dma((variables,)),
+            dma((PIECES,)),
             dma((3,)),
         ],
         compiler_params=pltpu.CompilerParams(

time: 36.8 us -> 36.6 us (level)
  no operation moved by 1% of the time
where the time goes in v4:
time: 36.6 us; the launch traced here: 36.5 us
  Pallas kernels  35.8 us (98%)
  between operations  0.64 us (2%)
    pallas_call x1, Pallas kernels, kernel_body(): pl.pallas_call(functools.partial(section_kernel, n), out_shape=(pltpu.VME...  35 us
    pallas_call x1, Pallas kernels, kernel_body(): pl.pallas_call(write_kernel, out_shape=(jax.ShapeDtypeStruct(flow_next.sh...  0.87 us

profile of v4, /device:TPU:0, one launch (start us, length us, event | category | flops | bytes accessed | tf_op | source)
XLA Modules:
  0.0 36.5 jit_solution(12917839201829541416)
XLA Ops:
  0.6 35.0 %section.1 = (f32[5,32,1024]{2,1,0:T(8,128)S(1)}, f32[5,32,128]{2,1,0:T(8,128)S(1)}) custom-call(f32[5,32,1024]{2,1,0:T(8,128)} %bitcast.3, f32[2,32,1024]{2,1,0:T(8,128)} %bitcast.4, f32[32,1024]{1,0:T(8,128)} %volume_hbm.1), custom_call_target="tpu_custom_call" | custom-call | tf_op jit(solution)/shard_map/section/pallas_call | solution.py:343
  35.6 0.9 %write.1 = (f32[5,32,1024]{2,1,0:T(8,128)}, f32[5,32,128]{2,1,0:T(8,128)}) custom-call(f32[5,32,1024]{2,1,0:T(8,128)S(1)} %get-tuple-element.6.next_ref, f32[5,32,128]{2,1,0:T(8,128)S(1)} %get-tuple-element.7.mean_ref), custom_call_target="tpu_custom_call" | custom-call | tf_op jit(solution)/shard_map/write/pallas_call | solution.py:374

commit v5 on v4

--- a/solution.py
+++ b/solution.py
@@ -197,24 +197,9 @@
     for s in range(1, n):
         pl.semaphore_signal(barrier, inc=1, device_id={"inst": peer(s)})
     pl.semaphore_signal(barrier, inc=1, device_id={"space": other})
-    for load in loads:
-        load.wait()
-    for edge, row in ((0, rows - 1), (1, 0)):
-        for v in range(variables):
-            edge_out[edge, v : v + 1, :] = flow_ref[v, row : row + 1, :]
-        for v in range(2):
-            edge_out[edge, variables + v : variables + v + 1, :] = grid_ref[v, row : row + 1, :]
-        edge_out[edge, variables + 2 : variables + 3, :] = jnp.zeros((1, columns), jnp.float32)
+    loads[0].wait()
     pl.semaphore_wait(barrier, n)
 
-    edges = pltpu.make_async_remote_copy(
-        src_ref=edge_out,
-        dst_ref=edge_in,
-        send_sem=edge_send,
-        recv_sem=edge_recv,
-        device_id={"space": other},
-    )
-    edges.start()
     cuts = [-(-variables * k // PIECES) for k in range(PIECES + 1)]
     pieces = list(enumerate(slice(a, b) for a, b in zip(cuts, cuts[1:])))
     for k, c in pieces:
@@ -227,6 +212,23 @@
                 device_id={"inst": peer(s)},
             ).start()
 
+    for load in loads[1:]:
+        load.wait()
+    for edge, row in ((0, rows - 1), (1, 0)):
+        for v in range(variables):
+            edge_out[edge, v : v + 1, :] = flow_ref[v, row : row + 1, :]
+        for v in range(2):
+            edge_out[edge, variables + v : variables + v + 1, :] = grid_ref[v, row : row + 1, :]
+        edge_out[edge, variables + 2 : variables + 3, :] = jnp.zeros((1, columns), jnp.float32)
+
+    edges = pltpu.make_async_remote_copy(
+        src_ref=edge_out,
+        dst_ref=edge_in,
+        send_sem=edge_send,
+        recv_sem=edge_recv,
+        device_id={"space": other},
+    )
+    edges.start()
     state = [flow_ref[v] for v in range(variables)]
     grid_0, grid_1, volume = grid_ref[0], grid_ref[1], volume_ref[...]
     speed_0, speed_1, pressure, sound = cell_terms(state)

time: 36.6 us -> 36.6 us (level)
  no operation moved by 1% of the time
where the time goes in v5:
time: 36.6 us; the launch traced here: 36.5 us
  Pallas kernels  35.8 us (98%)
  between operations  0.64 us (2%)
    pallas_call x1, Pallas kernels, kernel_body(): pl.pallas_call(functools.partial(section_kernel, n), out_shape=(pltpu.VME...  35 us
    pallas_call x1, Pallas kernels, kernel_body(): pl.pallas_call(write_kernel, out_shape=(jax.ShapeDtypeStruct(flow_next.sh...  0.87 us

profile of v5, /device:TPU:0, one launch (start us, length us, event | category | flops | bytes accessed | tf_op | source)
XLA Modules:
  0.0 36.5 jit_solution(5651740784022219169)
XLA Ops:
  0.6 35.0 %section.1 = (f32[5,32,1024]{2,1,0:T(8,128)S(1)}, f32[5,32,128]{2,1,0:T(8,128)S(1)}) custom-call(f32[5,32,1024]{2,1,0:T(8,128)} %bitcast.3, f32[2,32,1024]{2,1,0:T(8,128)} %bitcast.4, f32[32,1024]{1,0:T(8,128)} %volume_hbm.1), custom_call_target="tpu_custom_call" | custom-call | tf_op jit(solution)/shard_map/section/pallas_call | solution.py:345
  35.6 0.9 %write.1 = (f32[5,32,1024]{2,1,0:T(8,128)}, f32[5,32,128]{2,1,0:T(8,128)}) custom-call(f32[5,32,1024]{2,1,0:T(8,128)S(1)} %get-tuple-element.6.next_ref, f32[5,32,128]{2,1,0:T(8,128)S(1)} %get-tuple-element.7.mean_ref), custom_call_target="tpu_custom_call" | custom-call | tf_op jit(solution)/shard_map/write/pallas_call | solution.py:376
